TPU v7x, 1024 devices: a whole 8x8x8 slice. The times are simulated.
1024 devices in a mesh: px: 4 (over z_lo), py: 16 (over y, z_hi), depth: 16 (over x, core).
Axes of the slice: x: 8, y: 8, z: 8 (z_hi: 2, z_lo: 4; z = z_hi * 4 + z_lo), core: 2. Of those that a mesh axis runs over, the one named last changes fastest.
Arguments:
- tokens: bfloat16 [3072, 7168], P('depth', ('py', 'px')), may hold values from -6 to 6
- up_weight: bfloat16 [7168, 32768], P('py', ('px', 'depth')), may hold values from -0.1875 to 0.1875
- up_bias: bfloat16 [32768], P(('px', 'py')), may hold values from -3 to 3
Outputs:
- hidden: bfloat16 [3072, 32768], P('depth', ('px', 'py'))
All inputs are finite; a program needn't handle non-finite values.
Results may differ from a plain program's by a relative error of at most 0.022.
Values may be sent and summed in bfloat16 or wider, within the bound.
A program may use at most 32 MiB of HBM per device.

v0:
```python
import jax
import jax.numpy as jnp
from jax import lax
from jax.sharding import PartitionSpec as P


def body(tokens, up_weight, up_bias):
    features = lax.all_gather(tokens, "px", axis=1, tiled=True)
    partial_value = jnp.dot(
        features,
        lax.all_gather(up_weight, "depth", axis=1, tiled=True),
        preferred_element_type=jnp.float32,
    ).astype(jnp.bfloat16)
    summed = lax.psum_scatter(
        partial_value.astype(jnp.float32).astype(jnp.bfloat16),
        "py",
        scatter_dimension=1,
        tiled=True,
    ).astype(jnp.float32)
    summed = summed + up_bias.astype(jnp.float32)[None, :]
    return jax.nn.gelu(summed, approximate=True).astype(jnp.bfloat16)


def solution(mesh):
    return jax.shard_map(
        body,
        mesh=mesh,
        in_specs=(P("depth", ("py", "px")), P("py", ("px", "depth")), P(("px", "py"))),
        out_specs=P("depth", ("px", "py")),
        check_vma=False,
    )
```

profile of v0, /device:TPU:2, one launch (start us, length us, event | category | flops | bytes accessed | tf_op | source)
XLA Modules:
  0.0 331.8 jit_solution(13011479419442724877)
XLA Ops:
  6.5 0.0 all-gather.3.cloned.1.call-start
  6.5 0.7 all-gather.3.cloned.1.call-update
  7.3 0.0 reduce-scatter.2.cloned.1.call-start
  7.3 19.0 %all-gather = bf16[4,112,192]{1,2,0:T(8,128)(2,1)S(1)} all-gather(bf16[1,112,192]{1,2,0:T(8,128)(2,1)} %bitcast.7), channel_id=1, replica_groups=mesh['px'=4,'py'=16,'depth'=16] {'px'}, dimensions={0}, use_global_device_ids=true | all-gather | bytes 215040 | tf_op jit(solution)/shard_map/all_gather | solution.py:8
  26.3 0.2 copy.5
  26.4 0.2 reshape.2
  26.6 0.0 copy-start
  26.6 49.4 %all-gather.3.cloned.1.call-done = bf16[448,8192]{1,0:T(8,128)(2,1)} async-done(((bf16[448,512]{1,0:T(8,128)(2,1)}), bf16[448,8192]{1,0:T(8,128)(2,1)}) %all-gather.3.cloned.1.call-update) | async-done | bytes 7340048 | tf_op jit(solution)/shard_map/all_gather | solution.py:11
  76.0 6.6 %convolution_convert_fusion = bf16[192,8192]{1,0:T(8,128)(2,1)} fusion(bf16[448,192]{0,1:T(8,128)(2,1)S(1)} %reshape.2, bf16[448,8192]{1,0:T(8,128)(2,1)} %all-gather.3.cloned.1.call-done), kind=kOutput, calls=%fused_computation | convolution fusion | flops 1410859008 | bytes 10657792 | tf_op jit(solution)/shard_map/dot_general | solution.py:9
  82.6 0.0 reduce-scatter.2.cloned.1.call-update
  82.6 0.0 copy-done
  82.6 240.6 %reduce-scatter.2.cloned.1.call-done = bf16[192,512]{1,0:T(8,128)(2,1)} async-done(((bf16[192,8192]{1,0:T(8,128)(2,1)}), bf16[192,512]{1,0:T(8,128)(2,1)}) %reduce-scatter.2.cloned.1.call-update) | async-done | bytes 196624 | tf_op jit(solution)/shard_map/reduce_scatter | solution.py:14
  323.2 1.8 fusion.7
  (1 shorter events, 0.0 us)
Async XLA Ops:
  6.5 69.5 %all-gather.3.cloned.1.call-start = ((), (), s32[]{:S(2)}) async-start(), calls=%async_computation.1 | async-start | bytes 7798784 | tf_op jit(solution)/shard_map/all_gather | solution.py:11
  7.3 316.0 %reduce-scatter.2.cloned.1.call-start = ((), (), s32[]{:S(2)}) async-start(), calls=%async_computation.2 | async-start | bytes 3342336 | tf_op jit(solution)/shard_map/reduce_scatter | solution.py:14
  26.6 56.0 %copy-start = (bf16[512]{0:T(512)(128)(2,1)S(1)}, bf16[512]{0:T(512)(128)(2,1)}, u32[]{:S(2)}) copy-start(bf16[512]{0:T(512)(128)(2,1)} %param.5) | copy-start | bytes 3076
Sparse Core Ops, SparseCore 0:
  10.1 65.8 all-gather.2
  82.7 240.4 reduce-scatter.1
where the time goes:
time: 332 us
  waiting for transfers between devices  291 us (88%)
  blocking collectives  19 us (6%)
  between operations  13.4 us (4%)
  matrix products  6.59 us (2%)
    reduce_scatter x1, waiting for transfers between devices, body(): lax.psum_scatter(partial_value.astype(jnp.float32).astype(jnp.bfloat16),...  241 us
    all_gather x1, waiting for transfers between devices, body(): lax.all_gather(up_weight, 'depth', axis=1, tiled=True)  49.4 us
    all_gather x1, blocking collectives, body(): features = lax.all_gather(tokens, 'px', axis=1, tiled=True)  19 us
  transfers between devices with their start and end apart: 2, of which 2 were waited for; matrix products, arithmetic and copies ran while one was open for 0% of the time, Pallas kernels for 0%

commit v1 on v0

v1 whole, which is shorter than its diff:
```python
import jax
import jax.numpy as jnp
from jax import lax
from jax.experimental import pallas as pl
from jax.experimental.pallas import tpu as pltpu
from jax.sharding import PartitionSpec as P

MESH = pl.DeviceIdType.MESH
BF16, F32 = jnp.bfloat16, jnp.float32
N = 8
ROWS = 192
PIECES = 16
COLS = 256
HALF = 224
FEAT = 112
AHEAD = 8
LAG = 2


def device(x, core, y, z_hi, z_lo):
    return (z_lo, y * 2 + z_hi, x * 2 + core)


def piece_of(i):
    j = jnp.maximum(i - 2, 0)
    own = jnp.where(i < 2, 1, 0)
    hops = (1 - own) * (j // 4 + 1)
    r = j % 4
    far = hops // 4
    way = (1 - own) * (r % 2)
    half = own * i + (1 - own) * (far * r + (1 - far) * (r // 2))
    return hops, way, half


def kernel(
    t_ref, w_ref, b_ref, o_ref,
    t_in, t_cat, w_all, own_part, sib_out, sib_in, y_out, y_in, total,
    t_send, t_recv, swap_send, local_sem, w_send, w_recv, sib_send, sib_recv, y_send, y_recv,
):
    px, py, depth = lax.axis_index("px"), lax.axis_index("py"), lax.axis_index("depth")
    x, c = depth // 2, depth % 2
    y, zh, zl = py // 2, py % 2, px
    z = zh * 4 + zl
    near = jnp.where(c == zh, 1, 0)

    barrier = pltpu.get_barrier_semaphore()

    def greet(target):
        pl.semaphore_signal(barrier, inc=1, device_id=target, device_id_type=MESH)

    greet(device((x + 1) % N, c, y, zh, zl))
    greet(device((x + N - 1) % N, c, y, zh, zl))
    greet(device(x, 1 - c, y, zh, zl))
    greet(device(x, zh, y, 1 - zh, zl))
    for ct in range(2):
        for kz in range(2):
            for b in range(2):
                zl_from = 2 * c + b

                @pl.when((kz != zh) | (zl_from != zl))
                def _(ct=ct, kz=kz, zl_from=zl_from):
                    greet(device(x, ct, y, kz, zl_from))

    for dy in range(1, N):
        greet(device(x, c, (y + dy) % N, zh, zl))
    pl.semaphore_wait(barrier, 3 + 2 * (1 - near) + 7 + 7)

    def swap(h, q, remote):
        src = w_ref.at[pl.ds(h * HALF, HALF), pl.ds(q * COLS, COLS)]
        part = 1 - near
        dst = w_all.at[0, q, pl.ds(pl.multiple_of(part * HALF, HALF), HALF)]
        if remote:
            return pltpu.make_async_remote_copy(
                src_ref=src, dst_ref=dst, send_sem=swap_send.at[h, q], recv_sem=w_recv.at[0, part, q],
                device_id=device(x, h, y, c, zl), device_id_type=MESH)
        return pltpu.make_async_copy(src, dst, local_sem.at[q])

    def swap_all(run_remote, run_local):
        for q in range(2):
            for h in range(2):
                here = (c == zh) & (c == h)
                if run_local is not None:
                    @pl.when(here)
                    def _(h=h, q=q):
                        run_local(swap(h, q, False))

                @pl.when(jnp.logical_not(here))
                def _(h=h, q=q):
                    run_remote(swap(h, q, True))

    t_core = zl // 2
    b_mine = zl % 2

    def t_copy(dz):
        zd = (z + dz) % N
        zhd = zd // 4
        other = jnp.where(c == t_core, 0, 1)
        rel = jnp.where(zhd == zh, 0, 1)
        return pltpu.make_async_remote_copy(
            src_ref=t_ref, dst_ref=t_in.at[other, rel * 2 + b_mine], send_sem=t_send.at[dz],
            recv_sem=t_recv.at[other, rel * 2 + b_mine],
            device_id=device(x, t_core, y, zhd, zd % 4), device_id_type=MESH)

    def t_local():
        return pltpu.make_async_copy(t_ref, t_in.at[0, b_mine], local_sem.at[2])

    def send_tokens():
        for dz in (4, 3, 5, 2, 6, 1, 7):
            t_copy(dz).start()

        @pl.when(c != t_core)
        def _():
            t_copy(0).start()

        @pl.when(c == t_core)
        def _():
            t_local().start()

    @pl.when(c == zh)
    def _():
        swap_all(lambda d: d.start(), lambda d: d.start())
        send_tokens()

    @pl.when(c != zh)
    def _():
        send_tokens()
        swap_all(lambda d: d.start(), None)

    def w_copy(hops, way, part, half):
        rows = pl.ds(pl.multiple_of(part * HALF, HALF), HALF)
        slot = hops + 4 * way * jnp.where(hops > 0, 1, 0)
        to = hops + 1 + 4 * way
        return pltpu.make_async_remote_copy(
            src_ref=w_all.at[slot, half, rows], dst_ref=w_all.at[to, half, rows],
            send_sem=w_send.at[to, part, half], recv_sem=w_recv.at[to, part, half],
            device_id=device((x + 1 + 6 * way) % N, c, y, zh, zl), device_id_type=MESH)

    def w_arrived(slot, part, half):
        rows = pl.ds(pl.multiple_of(part * HALF, HALF), HALF)
        ref = w_all.at[slot, half, rows]
        pltpu.make_async_copy(ref, ref, w_recv.at[slot, part, half]).wait()

    def forward(i, part):
        hops, way, half = piece_of(i)
        slot = hops + 4 * way

        if part == 0:
            @pl.when((i < 2) & (c == zh))
            def _():
                ref = w_all.at[0, half, pl.ds(0, HALF)]
                pltpu.make_async_copy(ref, ref, local_sem.at[half]).wait()

            @pl.when((i >= 2) | (c != zh))
            def _():
                w_arrived(slot, 0, half)
        else:
            w_arrived(slot, 1, half)

        @pl.when((hops < 3) | ((hops == 3) & (half == way)))
        def _():
            w_copy(hops, way, part, half).start()

        @pl.when(hops == 0)
        def _():
            w_copy(hops, way + 1, part, half).start()

    def sib_copy(i):
        return pltpu.make_async_remote_copy(
            src_ref=sib_out.at[i], dst_ref=sib_in.at[i], send_sem=sib_send.at[i], recv_sem=sib_recv.at[i],
            device_id=device(x, 1 - c, y, zh, zl), device_id_type=MESH)

    def product(i):
        hops, way, half = piece_of(i)
        w = w_all[hops + 4 * way, half]
        sib_out[i] = jnp.dot(t_cat[1], w, preferred_element_type=F32).astype(BF16)
        sib_copy(i).start()
        own_part[i] = jnp.dot(t_cat[0], w, preferred_element_type=F32)

    def y_step(i):
        hops, way, half = piece_of(i)
        owner = (x + N + hops * (2 * way - 1)) % N
        return (owner + N - y) % N, half

    def y_copy(i, dy, half):
        return pltpu.make_async_remote_copy(
            src_ref=y_out.at[i], dst_ref=y_in.at[dy, half], send_sem=y_send.at[i], recv_sem=y_recv.at[dy, half],
            device_id=device(x, c, (y + dy) % N, zh, zl), device_id_type=MESH)

    def onward(i):
        sib_copy(i).wait_recv()
        dy, half = y_step(i)
        value = own_part[i] + sib_in[i].astype(F32)

        @pl.when(dy == 0)
        def _():
            total[half] = value

        @pl.when(dy != 0)
        def _():
            y_out[i] = value.astype(BF16)
            y_copy(i, dy, half).start()

    def lead(i, carry):
        forward(i, 0)
        return carry

    lax.fori_loop(0, AHEAD, lead, 0)

    for other in range(2):
        for s in range(4):
            mine = (other == 0) & (s == b_mine) & (c == t_core)

            @pl.when(mine)
            def _():
                t_local().wait()

            @pl.when(jnp.logical_not(mine))
            def _(other=other, s=s):
                ref = t_in.at[other, s]
                pltpu.make_async_copy(ref, ref, t_recv.at[other, s]).wait()

        t_cat[other] = jnp.concatenate([t_in[other, s] for s in range(4)], axis=-1)

    def step(i, carry):
        @pl.when(i < PIECES)
        def _():
            forward(i, 1)

        @pl.when(i + AHEAD < PIECES)
        def _():
            forward(i + AHEAD, 0)

        @pl.when(i < PIECES)
        def _():
            product(i)

        @pl.when(i >= LAG)
        def _():
            onward(i - LAG)

        return carry

    lax.fori_loop(0, PIECES + LAG, step, 0)

    def take(k, carry):
        dy, half = k // 2 + 1, k % 2
        ref = y_in.at[dy, half]
        pltpu.make_async_copy(ref, ref, y_recv.at[dy, half]).wait()
        return carry

    lax.fori_loop(0, 14, take, 0)
    for half in range(2):
        value = total[half]
        for dy in range(1, N):
            value = value + y_in[dy, half].astype(F32)
        value = value + b_ref[0:1, half * COLS:(half + 1) * COLS].astype(F32)
        inner = 0.7978845608028654 * (value + 0.044715 * (value * value * value))
        o_ref[:, half * COLS:(half + 1) * COLS] = (0.5 * value * (1.0 + jnp.tanh(inner))).astype(BF16)

    for dz in range(1, N):
        t_copy(dz).wait_send()

    @pl.when(c != t_core)
    def _():
        t_copy(0).wait_send()

    swap_all(lambda d: d.wait_send(), None)

    def done(i, carry):
        hops, way, half = piece_of(i)
        for part in range(2):
            @pl.when((hops < 3) | ((hops == 3) & (half == way)))
            def _():
                w_copy(hops, way, part, half).wait_send()

            @pl.when(hops == 0)
            def _():
                w_copy(hops, way + 1, part, half).wait_send()

        sib_copy(i).wait_send()
        dy, half = y_step(i)

        @pl.when(dy != 0)
        def _():
            y_copy(i, dy, half).wait_send()

        return carry

    lax.fori_loop(0, PIECES, done, 0)


def body(tokens, up_weight, up_bias):
    return pl.pallas_call(
        kernel,
        out_shape=jax.ShapeDtypeStruct((ROWS, 512), BF16),
        in_specs=[
            pl.BlockSpec(memory_space=pltpu.VMEM),
            pl.BlockSpec(memory_space=pltpu.VMEM),
            pl.BlockSpec(memory_space=pltpu.VMEM),
        ],
        out_specs=pl.BlockSpec(memory_space=pltpu.VMEM),
        scratch_shapes=[
            pltpu.VMEM((2, 4, ROWS, FEAT), BF16),
            pltpu.VMEM((2, ROWS, 4 * FEAT), BF16),
            pltpu.VMEM((9, 2, 2 * HALF, COLS), BF16),
            pltpu.VMEM((PIECES, ROWS, COLS), F32),
            pltpu.VMEM((PIECES, ROWS, COLS), BF16),
            pltpu.VMEM((PIECES, ROWS, COLS), BF16),
            pltpu.VMEM((PIECES, ROWS, COLS), BF16),
            pltpu.VMEM((N, 2, ROWS, COLS), BF16),
            pltpu.VMEM((2, ROWS, COLS), F32),
            pltpu.SemaphoreType.DMA((N,)),
            pltpu.SemaphoreType.DMA((2, 4)),
            pltpu.SemaphoreType.DMA((2, 2)),
            pltpu.SemaphoreType.DMA((3,)),
            pltpu.SemaphoreType.DMA((9, 2, 2)),
            pltpu.SemaphoreType.DMA((9, 2, 2)),
            pltpu.SemaphoreType.DMA((PIECES,)),
            pltpu.SemaphoreType.DMA((PIECES,)),
            pltpu.SemaphoreType.DMA((PIECES,)),
            pltpu.SemaphoreType.DMA((N, 2)),
        ],
        name="up_proj",
        compiler_params=pltpu.CompilerParams(
            collective_id=0, has_side_effects=True, vmem_limit_bytes=40 * 2**20
        ),
    )(tokens, up_weight, up_bias.reshape(1, 512))


def solution(mesh):
    return jax.shard_map(
        body,
        mesh=mesh,
        in_specs=(P("depth", ("py", "px")), P("py", ("px", "depth")), P(("px", "py"))),
        out_specs=P("depth", ("px", "py")),
        check_vma=False,
    )
```

time: 332 us -> 101 us (0.30)
  the two profiles are of different devices: /device:TPU:2 before, /device:TPU:119 now
where the time goes in v1:
time: 101 us
  Pallas kernels  97.3 us (96%)
  local copies, waits for them, and re-layouts  3.18 us (3%)
    pallas_call x1, Pallas kernels, body(): pl.pallas_call(kernel, out_shape=jax.ShapeDtypeStruct((ROWS, 512), BF16),...  97.3 us
    unnamed x5, local copies, waits for them, and re-layouts  2.5 us

profile of v1, /device:TPU:119, one launch (start us, length us, event | category | flops | bytes accessed | tf_op | source)
XLA Modules:
  0.0 100.5 jit_solution(17599306143220856249)
XLA Ops:
  0.0 0.7 reshape.3.b_ref
  0.7 0.0 copy-start
  0.7 1.0 %copy-done = bf16[448,512]{1,0:T(8,128)(2,1)S(1)} copy-done((bf16[448,512]{1,0:T(8,128)(2,1)S(1)}, bf16[448,512]{1,0:T(8,128)(2,1)}, u32[]{:S(2)}) %copy-start) | copy-done | bytes 458776
  1.7 0.0 copy-start.1
  1.7 0.8 copy-done.1
  2.5 97.3 %up_proj.1 = bf16[192,512]{1,0:T(8,128)(2,1)S(1)} custom-call(bf16[192,112]{1,0:T(8,128)(2,1)S(1)} %copy-done.1, bf16[448,512]{1,0:T(8,128)(2,1)S(1)} %copy-done, bf16[1,512]{1,0:T(2,128)(2,1)S(1)} %reshape.3.b_ref), custom_call_target="tpu_custom_call" | custom-call | tf_op jit(solution)/shard_map/up_proj/pallas_call | solution.py:293
  99.8 0.7 copy.5
Async XLA Ops:
  0.7 1.0 %copy-start = (bf16[448,512]{1,0:T(8,128)(2,1)S(1)}, bf16[448,512]{1,0:T(8,128)(2,1)}, u32[]{:S(2)}) copy-start(bf16[448,512]{1,0:T(8,128)(2,1)} %w_ref.1) | copy-start | bytes 1376260
  1.7 0.8 copy-start.1

commit v2 on v1

v2 whole, which is shorter than its diff:
```python
import jax
import jax.numpy as jnp
from jax import lax
from jax.experimental import pallas as pl
from jax.experimental.pallas import tpu as pltpu
from jax.sharding import PartitionSpec as P

MESH = pl.DeviceIdType.MESH
BF16, F32 = jnp.bfloat16, jnp.float32
N = 8
ROWS = 192
PIECES = 16
COLS = 256
HALF = 224
FEAT = 112
NEAR_AT, FAR_AT, PRODUCT_AT, PAIR_AT, JOIN_AT, OWNER_AT = 0, 8, 11, 13, 20, 28
TOKENS_AT = 9


def device(x, core, y, z_hi, z_lo):
    return (z_lo, y * 2 + z_hi, x * 2 + core)


def piece_of(i):
    if i < 2:
        return 0, 0, i
    hops, r = (i - 2) // 4 + 1, (i - 2) % 4
    return hops, r % 2, r if hops == 4 else r // 2


def kernel(
    t_ref, w_ref, b_ref, o_ref,
    t_in, t_cat, w_all, own_part, sib_out, sib_in, y_out, y_in,
    t_send, t_recv, swap_send, local_sem, w_send, w_recv, sib_send, sib_recv, y_send, y_recv,
):
    px, py, depth = lax.axis_index("px"), lax.axis_index("py"), lax.axis_index("depth")
    x, c = depth // 2, depth % 2
    y, zh, zl = py // 2, py % 2, px
    z = zh * 4 + zl
    x_right, x_left = (x + 1) % N, (x + N - 1) % N
    near = jnp.where(c == zh, 1, 0)

    barrier = pltpu.get_barrier_semaphore()

    def greet(target):
        pl.semaphore_signal(barrier, inc=1, device_id=target, device_id_type=MESH)

    greet(device((x + 1) % N, c, y, zh, zl))
    greet(device((x + N - 1) % N, c, y, zh, zl))
    greet(device(x, 1 - c, y, zh, zl))
    greet(device(x, zh, y, 1 - zh, zl))
    for ct in range(2):
        for kz in range(2):
            for b in range(2):
                zl_from = 2 * c + b

                @pl.when((kz != zh) | (zl_from != zl))
                def _(ct=ct, kz=kz, zl_from=zl_from):
                    greet(device(x, ct, y, kz, zl_from))

    for dy in (1, 2, 6, 7):
        greet(device(x, c, (y + dy) % N, zh, zl))
    pl.semaphore_wait(barrier, 3 + 2 * (1 - near) + 7 + 4)

    def swap(h, q, remote):
        src = w_ref.at[pl.ds(h * HALF, HALF), pl.ds(q * COLS, COLS)]
        part = 1 - near
        dst = w_all.at[0, q, pl.ds(pl.multiple_of(part * HALF, HALF), HALF)]
        if remote:
            return pltpu.make_async_remote_copy(
                src_ref=src, dst_ref=dst, send_sem=swap_send.at[h, q], recv_sem=w_recv.at[0, part, q],
                device_id=device(x, h, y, c, zl), device_id_type=MESH)
        return pltpu.make_async_copy(src, dst, local_sem.at[q])

    def swap_all(run_remote, run_local):
        for q in range(2):
            for h in range(2):
                here = (c == zh) & (c == h)
                if run_local is not None:
                    @pl.when(here)
                    def _(h=h, q=q):
                        run_local(swap(h, q, False))

                @pl.when(jnp.logical_not(here))
                def _(h=h, q=q):
                    run_remote(swap(h, q, True))

    t_core = zl // 2
    b_mine = zl % 2

    def t_copy(dz):
        zd = (z + dz) % N
        zhd = zd // 4
        other = jnp.where(c == t_core, 0, 1)
        rel = jnp.where(zhd == zh, 0, 1)
        return pltpu.make_async_remote_copy(
            src_ref=t_ref, dst_ref=t_in.at[other, rel * 2 + b_mine], send_sem=t_send.at[dz],
            recv_sem=t_recv.at[other, rel * 2 + b_mine],
            device_id=device(x, t_core, y, zhd, zd % 4), device_id_type=MESH)

    def t_local():
        return pltpu.make_async_copy(t_ref, t_in.at[0, b_mine], local_sem.at[2])

    def send_tokens():
        for dz in (4, 3, 5, 2, 6, 1, 7):
            t_copy(dz).start()

        @pl.when(c != t_core)
        def _():
            t_copy(0).start()

        @pl.when(c == t_core)
        def _():
            t_local().start()

    swap_all(lambda d: d.start(), lambda d: d.start())

    def w_copy(hops, way, part, half):
        rows = pl.ds(part * HALF, HALF)
        slot = hops + 4 * way if hops else 0
        to = hops + 1 + 4 * way
        return pltpu.make_async_remote_copy(
            src_ref=w_all.at[slot, half, rows], dst_ref=w_all.at[to, half, rows],
            send_sem=w_send.at[to, part, half], recv_sem=w_recv.at[to, part, half],
            device_id=device(x_left if way else x_right, c, y, zh, zl), device_id_type=MESH)

    def w_arrived(slot, part, half):
        ref = w_all.at[slot, half, pl.ds(part * HALF, HALF)]
        pltpu.make_async_copy(ref, ref, w_recv.at[slot, part, half]).wait()

    def onward_ways(hops, way, half):
        if hops == 0:
            return (0, 1)
        return (way,) if hops < 3 or (hops == 3 and half == way) else ()

    def forward(i, part):
        hops, way, half = piece_of(i)
        slot = hops + 4 * way

        if part == 0 and i < 2:
            @pl.when(c == zh)
            def _():
                ref = w_all.at[0, half, pl.ds(0, HALF)]
                pltpu.make_async_copy(ref, ref, local_sem.at[half]).wait()

            @pl.when(c != zh)
            def _():
                w_arrived(slot, 0, half)
        else:
            w_arrived(slot, part, half)
        for leave in onward_ways(hops, way, half):
            w_copy(hops, leave, part, half).start()

    def sib_copy(i):
        return pltpu.make_async_remote_copy(
            src_ref=sib_out.at[i], dst_ref=sib_in.at[i], send_sem=sib_send.at[i], recv_sem=sib_recv.at[i],
            device_id=device(x, 1 - c, y, zh, zl), device_id_type=MESH)

    def product(i):
        hops, way, half = piece_of(i)
        w = w_all[hops + 4 * way, half]
        sib_out[i] = jnp.dot(t_cat[1], w, preferred_element_type=F32).astype(BF16)
        sib_copy(i).start()
        own_part[i] = jnp.dot(t_cat[0], w, preferred_element_type=F32)

    def y_role(i):
        hops, way, half = piece_of(i)
        owner = (x + N + hops * (2 * way - 1)) % N
        return (N + (y - owner) * (1 - 2 * half)) % N, half

    def pass_on(i, role, half):
        to_second = jnp.where((role == 3) | (role == 7), 1, 0)
        step = jnp.where(role == 3, -2, jnp.where(role >= 5, 1, -1)) * (1 - 2 * half)
        return pltpu.make_async_remote_copy(
            src_ref=y_out.at[i], dst_ref=y_in.at[i, to_second], send_sem=y_send.at[i], recv_sem=y_recv.at[i, to_second],
            device_id=device(x, c, (y + N + step) % N, zh, zl), device_id_type=MESH)

    def received(i, k):
        ref = y_in.at[i, k]
        pltpu.make_async_copy(ref, ref, y_recv.at[i, k]).wait()
        return y_in[i, k].astype(F32)

    def pair_step(i):
        sib_copy(i).wait_recv()
        role, half = y_role(i)
        value = own_part[i] + sib_in[i].astype(F32)
        leaf = (role == 4) | (role == 2) | (role == 5)

        @pl.when(leaf)
        def _():
            y_out[i] = value.astype(BF16)
            pass_on(i, role, half).start()

        @pl.when(jnp.logical_not(leaf))
        def _():
            own_part[i] = value

    def join_step(i):
        role, half = y_role(i)

        @pl.when((role == 3) | (role == 6))
        def _():
            y_out[i] = (own_part[i] + received(i, 0)).astype(BF16)
            pass_on(i, role, half).start()

    def owner_step(i):
        role, half = y_role(i)

        @pl.when((role == 1) | (role == 7))
        def _():
            value = own_part[i] + received(i, 0)

            @pl.when(role == 1)
            def _():
                y_out[i] = (value + received(i, 1)).astype(BF16)

            @pl.when(role == 7)
            def _():
                y_out[i] = value.astype(BF16)

            pass_on(i, role, half).start()

    def result(i):
        role, half = y_role(i)

        @pl.when(role == 0)
        def _():
            value = own_part[i] + received(i, 0) + received(i, 1)
            value = value + b_ref[half * COLS:(half + 1) * COLS].astype(F32)[None, :]
            inner = 0.7978845608028654 * (value + 0.044715 * (value * value * value))
            o_ref[:, half * COLS:(half + 1) * COLS] = (0.5 * value * (1.0 + jnp.tanh(inner))).astype(BF16)

    def take_tokens():
        for other in range(2):
            for s in range(4):
                mine = (other == 0) & (s == b_mine) & (c == t_core)

                @pl.when(mine)
                def _():
                    t_local().wait()

                @pl.when(jnp.logical_not(mine))
                def _(other=other, s=s):
                    ref = t_in.at[other, s]
                    pltpu.make_async_copy(ref, ref, t_recv.at[other, s]).wait()

            t_cat[other] = jnp.concatenate([t_in[other, s] for s in range(4)], axis=-1)

    for t in range(PIECES + OWNER_AT):
        for offset, act in (
            (NEAR_AT, lambda i: forward(i, 0)),
            (FAR_AT, lambda i: forward(i, 1)),
            (PRODUCT_AT, product),
            (PAIR_AT, pair_step),
            (JOIN_AT, join_step),
            (OWNER_AT, owner_step),
        ):
            if act is product and t == PRODUCT_AT:
                take_tokens()
            if offset <= t < offset + PIECES:
                act(t - offset)
        if t == TOKENS_AT:
            send_tokens()

    for dz in range(1, N):
        t_copy(dz).wait_send()

    @pl.when(c != t_core)
    def _():
        t_copy(0).wait_send()

    swap_all(lambda d: d.wait_send(), None)

    for i in range(PIECES):
        hops, way, half = piece_of(i)
        for part in range(2):
            for leave in onward_ways(hops, way, half):
                w_copy(hops, leave, part, half).wait_send()
        sib_copy(i).wait_send()
        role, half = y_role(i)

        @pl.when(role != 0)
        def _():
            pass_on(i, role, half).wait_send()

    for i in range(PIECES):
        result(i)


def body(tokens, up_weight, up_bias):
    return pl.pallas_call(
        kernel,
        out_shape=jax.ShapeDtypeStruct((ROWS, 512), BF16),
        in_specs=[
            pl.BlockSpec(memory_space=pltpu.HBM),
            pl.BlockSpec(memory_space=pltpu.HBM),
            pl.BlockSpec(memory_space=pltpu.VMEM),
        ],
        out_specs=pl.BlockSpec(memory_space=pltpu.VMEM),
        scratch_shapes=[
            pltpu.VMEM((2, 4, ROWS, FEAT), BF16),
            pltpu.VMEM((2, ROWS, 4 * FEAT), BF16),
            pltpu.VMEM((9, 2, 2 * HALF, COLS), BF16),
            pltpu.VMEM((PIECES, ROWS, COLS), F32),
            pltpu.VMEM((PIECES, ROWS, COLS), BF16),
            pltpu.VMEM((PIECES, ROWS, COLS), BF16),
            pltpu.VMEM((PIECES, ROWS, COLS), BF16),
            pltpu.VMEM((PIECES, 2, ROWS, COLS), BF16),
            pltpu.SemaphoreType.DMA((N,)),
            pltpu.SemaphoreType.DMA((2, 4)),
            pltpu.SemaphoreType.DMA((2, 2)),
            pltpu.SemaphoreType.DMA((3,)),
            pltpu.SemaphoreType.DMA((9, 2, 2)),
            pltpu.SemaphoreType.DMA((9, 2, 2)),
            pltpu.SemaphoreType.DMA((PIECES,)),
            pltpu.SemaphoreType.DMA((PIECES,)),
            pltpu.SemaphoreType.DMA((PIECES,)),
            pltpu.SemaphoreType.DMA((PIECES, 2)),
        ],
        name="up_proj",
        compiler_params=pltpu.CompilerParams(
            collective_id=0, has_side_effects=True, vmem_limit_bytes=40 * 2**20
        ),
    )(tokens, up_weight, up_bias)


def solution(mesh):
    return jax.shard_map(
        body,
        mesh=mesh,
        in_specs=(P("depth", ("py", "px")), P("py", ("px", "depth")), P(("px", "py"))),
        out_specs=P("depth", ("px", "py")),
        check_vma=False,
    )
```

time: 101 us -> 86.4 us (0.86)
  the two profiles are of different devices: /device:TPU:119 before, /device:TPU:6 now
where the time goes in v2:
time: 86.4 us; the launch traced here: 86.2 us
  Pallas kernels  83 us (96%)
  local copies, waits for them, and re-layouts  3.17 us (4%)
    pallas_call x1, Pallas kernels, body(): pl.pallas_call(kernel, out_shape=jax.ShapeDtypeStruct((ROWS, 512), BF16),...  83 us
    unnamed x7, local copies, waits for them, and re-layouts  3.17 us

profile of v2, /device:TPU:6, one launch (start us, length us, event | category | flops | bytes accessed | tf_op | source)
XLA Modules:
  0.0 86.2 jit_solution(15006754969025321554)
XLA Ops:
  0.0 0.0 copy-start
  0.0 1.0 %copy-done = bf16[448,512]{1,0:T(8,128)(2,1)S(1)} copy-done((bf16[448,512]{1,0:T(8,128)(2,1)S(1)}, bf16[448,512]{1,0:T(8,128)(2,1)}, u32[]{:S(2)}) %copy-start) | copy-done | bytes 458776
  1.0 0.0 copy-start.1
  1.0 0.8 copy-done.1
  1.8 0.0 copy-start.2
  1.8 0.7 copy-done.2
  2.5 83.0 %up_proj.1 = bf16[192,512]{1,0:T(8,128)(2,1)S(1)} custom-call(bf16[192,112]{1,0:T(8,128)(2,1)S(1)} %copy-done.1, bf16[448,512]{1,0:T(8,128)(2,1)S(1)} %copy-done, bf16[512]{0:T(512)(128)(2,1)S(1)} %copy-done.2), custom_call_target="tpu_custom_call" | custom-call | tf_op jit(solution)/shard_map/up_proj/pallas_call | solution.py:291
  85.5 0.7 copy.5
Async XLA Ops:
  0.0 1.0 %copy-start = (bf16[448,512]{1,0:T(8,128)(2,1)S(1)}, bf16[448,512]{1,0:T(8,128)(2,1)}, u32[]{:S(2)}) copy-start(bf16[448,512]{1,0:T(8,128)(2,1)} %w_ref.1) | copy-start | bytes 1376260
  1.0 0.8 copy-start.1
  1.8 0.7 copy-start.2

commit v3 on v2

--- a/solution.py
+++ b/solution.py
@@ -13,8 +13,23 @@
 COLS = 256
 HALF = 224
 FEAT = 112
-NEAR_AT, FAR_AT, PRODUCT_AT, PAIR_AT, JOIN_AT, OWNER_AT = 0, 8, 11, 13, 20, 28
-TOKENS_AT = 9
+PART = 96
+STEPS = (
+    0, 1, 2, 5, 4, 3, 16, 96, 6, 17, 9, 18, 8, 7, 10, 19, 97, 34, 20, 35,
+    21, 11, 33, 32, 12, 37, 36, 23, 51, 22, 49, 38, 53, 50, 48, 13, 52, 39, 54, 24,
+    55, 40, 25, 26, 42, 56, 41, 67, 27, 43, 66, 71, 15, 14, 70, 57, 58, 64, 65, 28,
+    59, 44, 29, 30, 45, 46, 60, 68, 61, 62, 86, 75, 72, 87, 31, 47, 74, 73, 63, 76,
+    84, 69, 77, 78, 88, 83, 80, 89, 85, 79, 82, 81,
+)
+DEEP = {
+    4: (1, -1, 0, 0), 2: (1, -1, 0, 0), 5: (1, 1, 0, 0),
+    3: (2, -2, 1, 1), 6: (2, 1, 0, 1), 1: (3, -1, 0, 2), 7: (3, 1, 1, 1),
+}
+FLAT = {
+    4: (1, -1, 0, 0), 2: (1, -1, 0, 0), 5: (1, 1, 0, 0), 7: (1, 1, 2, 0),
+    3: (2, -3, 0, 1), 6: (2, 2, 3, 1), 1: (2, -1, 1, 1),
+}
+DEEP_PIECES = 10
 
 
 def device(x, core, y, z_hi, z_lo):
@@ -58,9 +73,9 @@
                 def _(ct=ct, kz=kz, zl_from=zl_from):
                     greet(device(x, ct, y, kz, zl_from))
 
-    for dy in (1, 2, 6, 7):
+    for dy in (1, 2, 3, 5, 6, 7):
         greet(device(x, c, (y + dy) % N, zh, zl))
-    pl.semaphore_wait(barrier, 3 + 2 * (1 - near) + 7 + 4)
+    pl.semaphore_wait(barrier, 3 + 2 * (1 - near) + 7 + 6)
 
     def swap(h, q, remote):
         src = w_ref.at[pl.ds(h * HALF, HALF), pl.ds(q * COLS, COLS)]
@@ -163,72 +178,84 @@
         sib_copy(i).start()
         own_part[i] = jnp.dot(t_cat[0], w, preferred_element_type=F32)
 
-    def y_role(i):
+    def tree_of(i):
+        return DEEP if i < DEEP_PIECES else FLAT
+
+    def climb(i, u, role):
+        step, slot = 0, 0
+        for r, (_, r_step, r_slot, _) in tree_of(i).items():
+            step = jnp.where(role == r, r_step, step)
+            slot = jnp.where(role == r, r_slot, slot)
+        return pltpu.make_async_remote_copy(
+            src_ref=y_out.at[i, u], dst_ref=y_in.at[i, slot, u],
+            send_sem=y_send.at[i, u], recv_sem=y_recv.at[i, slot, u],
+            device_id=device(x, c, (y + N + step * (1 - 2 * u)) % N, zh, zl), device_id_type=MESH)
+
+    def role_of(i, u):
         hops, way, half = piece_of(i)
         owner = (x + N + hops * (2 * way - 1)) % N
-        return (N + (y - owner) * (1 - 2 * half)) % N, half
-
-    def pass_on(i, role, half):
-        to_second = jnp.where((role == 3) | (role == 7), 1, 0)
-        step = jnp.where(role == 3, -2, jnp.where(role >= 5, 1, -1)) * (1 - 2 * half)
-        return pltpu.make_async_remote_copy(
-            src_ref=y_out.at[i], dst_ref=y_in.at[i, to_second], send_sem=y_send.at[i], recv_sem=y_recv.at[i, to_second],
-            device_id=device(x, c, (y + N + step) % N, zh, zl), device_id_type=MESH)
-
-    def received(i, k):
-        ref = y_in.at[i, k]
-        pltpu.make_async_copy(ref, ref, y_recv.at[i, k]).wait()
-        return y_in[i, k].astype(F32)
+        return (N + (y - owner) * (1 - 2 * u)) % N
+
+    def received(i, k, u):
+        ref = y_in.at[i, k, u]
+        pltpu.make_async_copy(ref, ref, y_recv.at[i, k, u]).wait()
+        return y_in[i, k, u].astype(F32)
+
+    def any_of(role, roles):
+        hit = role == roles[0]
+        for r in roles[1:]:
+            hit = hit | (role == r)
+        return hit
 
     def pair_step(i):
         sib_copy(i).wait_recv()
-        role, half = y_role(i)
-        value = own_part[i] + sib_in[i].astype(F32)
-        leaf = (role == 4) | (role == 2) | (role == 5)
-
-        @pl.when(leaf)
+        leaves = [r for r, v in tree_of(i).items() if v[0] == 1]
+        for u in range(2):
+            role = role_of(i, u)
+            rows = slice(u * PART, (u + 1) * PART)
+            value = own_part[i, rows] + sib_in[i, rows].astype(F32)
+            leaf = any_of(role, leaves)
+
+            @pl.when(leaf)
+            def _():
+                y_out[i, u] = value.astype(BF16)
+                climb(i, u, role).start()
+
+            @pl.when(jnp.logical_not(leaf))
+            def _():
+                own_part[i, rows] = value
+
+    def tree_step(i, level):
+        for u in range(2):
+            role = role_of(i, u)
+            rows = slice(u * PART, (u + 1) * PART)
+            for count in (1, 2):
+                roles = [r for r, v in tree_of(i).items() if v[0] == level and v[3] == count]
+                if not roles:
+                    continue
+
+                @pl.when(any_of(role, roles))
+                def _(count=count):
+                    value = own_part[i, rows]
+                    for k in range(count):
+                        value = value + received(i, k, u)
+                    y_out[i, u] = value.astype(BF16)
+                    climb(i, u, role).start()
+
+    def result(i):
+        _, _, half = piece_of(i)
+        cols = slice(half * COLS, (half + 1) * COLS)
+
+        @pl.when(role_of(i, 0) == 0)
         def _():
-            y_out[i] = value.astype(BF16)
-            pass_on(i, role, half).start()
-
-        @pl.when(jnp.logical_not(leaf))
-        def _():
-            own_part[i] = value
-
-    def join_step(i):
-        role, half = y_role(i)
-
-        @pl.when((role == 3) | (role == 6))
-        def _():
-            y_out[i] = (own_part[i] + received(i, 0)).astype(BF16)
-            pass_on(i, role, half).start()
-
-    def owner_step(i):
-        role, half = y_role(i)
-
-        @pl.when((role == 1) | (role == 7))
-        def _():
-            value = own_part[i] + received(i, 0)
-
-            @pl.when(role == 1)
-            def _():
-                y_out[i] = (value + received(i, 1)).astype(BF16)
-
-            @pl.when(role == 7)
-            def _():
-                y_out[i] = value.astype(BF16)
-
-            pass_on(i, role, half).start()
-
-    def result(i):
-        role, half = y_role(i)
-
-        @pl.when(role == 0)
-        def _():
-            value = own_part[i] + received(i, 0) + received(i, 1)
-            value = value + b_ref[half * COLS:(half + 1) * COLS].astype(F32)[None, :]
-            inner = 0.7978845608028654 * (value + 0.044715 * (value * value * value))
-            o_ref[:, half * COLS:(half + 1) * COLS] = (0.5 * value * (1.0 + jnp.tanh(inner))).astype(BF16)
+            for u in range(2):
+                rows = slice(u * PART, (u + 1) * PART)
+                value = own_part[i, rows]
+                for k in range(2 if i < DEEP_PIECES else 4):
+                    value = value + received(i, k, u)
+                value = value + b_ref[cols].astype(F32)[None, :]
+                inner = 0.7978845608028654 * (value + 0.044715 * (value * value * value))
+                o_ref[rows, cols] = (0.5 * value * (1.0 + jnp.tanh(inner))).astype(BF16)
 
     def take_tokens():
         for other in range(2):
@@ -246,21 +273,20 @@
 
             t_cat[other] = jnp.concatenate([t_in[other, s] for s in range(4)], axis=-1)
 
-    for t in range(PIECES + OWNER_AT):
-        for offset, act in (
-            (NEAR_AT, lambda i: forward(i, 0)),
-            (FAR_AT, lambda i: forward(i, 1)),
-            (PRODUCT_AT, product),
-            (PAIR_AT, pair_step),
-            (JOIN_AT, join_step),
-            (OWNER_AT, owner_step),
-        ):
-            if act is product and t == PRODUCT_AT:
-                take_tokens()
-            if offset <= t < offset + PIECES:
-                act(t - offset)
-        if t == TOKENS_AT:
+    for code in STEPS:
+        kind, i = code // 16, code % 16
+        if kind < 2:
+            forward(i, kind)
+        elif kind == 2:
+            product(i)
+        elif kind == 3:
+            pair_step(i)
+        elif kind < 6:
+            tree_step(i, kind - 2)
+        elif i == 0:
             send_tokens()
+        else:
+            take_tokens()
 
     for dz in range(1, N):
         t_copy(dz).wait_send()
@@ -277,11 +303,12 @@
             for leave in onward_ways(hops, way, half):
                 w_copy(hops, leave, part, half).wait_send()
         sib_copy(i).wait_send()
-        role, half = y_role(i)
-
-        @pl.when(role != 0)
-        def _():
-            pass_on(i, role, half).wait_send()
+        for u in range(2):
+            role = role_of(i, u)
+
+            @pl.when(role != 0)
+            def _():
+                climb(i, u, role).wait_send()
 
     for i in range(PIECES):
         result(i)
@@ -304,8 +331,8 @@
             pltpu.VMEM((PIECES, ROWS, COLS), F32),
             pltpu.VMEM((PIECES, ROWS, COLS), BF16),
             pltpu.VMEM((PIECES, ROWS, COLS), BF16),
-            pltpu.VMEM((PIECES, ROWS, COLS), BF16),
-            pltpu.VMEM((PIECES, 2, ROWS, COLS), BF16),
+            pltpu.VMEM((PIECES, 2, PART, COLS), BF16),
+            pltpu.VMEM((PIECES, 4, 2, PART, COLS), BF16),
             pltpu.SemaphoreType.DMA((N,)),
             pltpu.SemaphoreType.DMA((2, 4)),
             pltpu.SemaphoreType.DMA((2, 2)),
@@ -314,8 +341,8 @@
             pltpu.SemaphoreType.DMA((9, 2, 2)),
             pltpu.SemaphoreType.DMA((PIECES,)),
             pltpu.SemaphoreType.DMA((PIECES,)),
-            pltpu.SemaphoreType.DMA((PIECES,)),
             pltpu.SemaphoreType.DMA((PIECES, 2)),
+            pltpu.SemaphoreType.DMA((PIECES, 4, 2)),
         ],
         name="up_proj",
         compiler_params=pltpu.CompilerParams(

time: 86.4 us -> 83.6 us (0.968)
  the two profiles are of different devices: /device:TPU:6 before, /device:TPU:8 now
where the time goes in v3:
time: 83.6 us; the launch traced here: 83.4 us
  Pallas kernels  80.2 us (96%)
  local copies, waits for them, and re-layouts  3.17 us (4%)
    pallas_call x1, Pallas kernels, body(): pl.pallas_call(kernel, out_shape=jax.ShapeDtypeStruct((ROWS, 512), BF16),...  80.2 us
    unnamed x7, local copies, waits for them, and re-layouts  3.17 us

profile of v3, /device:TPU:8, one launch (start us, length us, event | category | flops | bytes accessed | tf_op | source)
XLA Modules:
  0.0 83.4 jit_solution(12281927553450738719)
XLA Ops:
  0.0 0.0 copy-start
  0.0 1.0 %copy-done = bf16[448,512]{1,0:T(8,128)(2,1)S(1)} copy-done((bf16[448,512]{1,0:T(8,128)(2,1)S(1)}, bf16[448,512]{1,0:T(8,128)(2,1)}, u32[]{:S(2)}) %copy-start) | copy-done | bytes 458776
  1.0 0.0 copy-start.1
  1.0 0.8 copy-done.1
  1.8 0.0 copy-start.2
  1.8 0.7 copy-done.2
  2.5 80.2 %up_proj.1 = bf16[192,512]{1,0:T(8,128)(2,1)S(1)} custom-call(bf16[192,112]{1,0:T(8,128)(2,1)S(1)} %copy-done.1, bf16[448,512]{1,0:T(8,128)(2,1)S(1)} %copy-done, bf16[512]{0:T(512)(128)(2,1)S(1)} %copy-done.2), custom_call_target="tpu_custom_call" | custom-call | tf_op jit(solution)/shard_map/up_proj/pallas_call | solution.py:318
  82.7 0.7 copy.5
Async XLA Ops:
  0.0 1.0 %copy-start = (bf16[448,512]{1,0:T(8,128)(2,1)S(1)}, bf16[448,512]{1,0:T(8,128)(2,1)}, u32[]{:S(2)}) copy-start(bf16[448,512]{1,0:T(8,128)(2,1)} %w_ref.1) | copy-start | bytes 1376260
  1.0 0.8 copy-start.1
  1.8 0.7 copy-start.2

commit v4 on v3

--- a/solution.py
+++ b/solution.py
@@ -15,11 +15,11 @@
 FEAT = 112
 PART = 96
 STEPS = (
-    0, 1, 2, 5, 4, 3, 16, 96, 6, 17, 9, 18, 8, 7, 10, 19, 97, 34, 20, 35,
-    21, 11, 33, 32, 12, 37, 36, 23, 51, 22, 49, 38, 53, 50, 48, 13, 52, 39, 54, 24,
-    55, 40, 25, 26, 42, 56, 41, 67, 27, 43, 66, 71, 15, 14, 70, 57, 58, 64, 65, 28,
-    59, 44, 29, 30, 45, 46, 60, 68, 61, 62, 86, 75, 72, 87, 31, 47, 74, 73, 63, 76,
-    84, 69, 77, 78, 88, 83, 80, 89, 85, 79, 82, 81,
+    1, 0, 3, 4, 5, 2, 17, 16, 96, 6, 9, 7, 8, 18, 19, 10, 97, 32, 33, 34,
+    12, 35, 20, 36, 21, 50, 13, 23, 22, 37, 39, 38, 48, 49, 51, 52, 11, 53, 14, 55,
+    54, 24, 26, 40, 42, 25, 27, 71, 15, 66, 67, 41, 65, 70, 64, 43, 58, 57, 56, 68,
+    69, 59, 28, 44, 29, 30, 45, 46, 87, 60, 61, 62, 86, 74, 72, 31, 80, 83, 47, 82,
+    73, 81, 75, 84, 63, 76, 77, 78, 85, 88, 89, 79,
 )
 DEEP = {
     4: (1, -1, 0, 0), 2: (1, -1, 0, 0), 5: (1, 1, 0, 0),
@@ -346,7 +346,7 @@
         ],
         name="up_proj",
         compiler_params=pltpu.CompilerParams(
-            collective_id=0, has_side_effects=True, vmem_limit_bytes=40 * 2**20
+            collective_id=0, has_side_effects=True, vmem_limit_bytes=60 * 2**20
         ),
     )(tokens, up_weight, up_bias)
 

time: 83.6 us -> 86.7 us (1.037)
  Pallas kernels: 80.2 us -> 84.8 us
  local copies, waits for them, and re-layouts: 3.17 us -> 1.62 us
    pallas_call x1, Pallas kernels: 80.2 us -> 84.8 us  [body(): pl.pallas_call(kernel, out_shape=jax.ShapeDtypeStruct((ROWS, 512), BF16),...]
    unnamed x7 -> x1, local copies, waits for them, and re-layouts: 3.17 us -> 1.62 us
where the time goes in v4:
time: 86.7 us; the launch traced here: 86.5 us
  Pallas kernels  84.8 us (98%)
  local copies, waits for them, and re-layouts  1.62 us (2%)
    pallas_call x1, Pallas kernels, body(): pl.pallas_call(kernel, out_shape=jax.ShapeDtypeStruct((ROWS, 512), BF16),...  84.8 us

profile of v4, /device:TPU:8, one launch (start us, length us, event | category | flops | bytes accessed | tf_op | source)
XLA Modules:
  0.0 86.5 jit_solution(14830009925057341901)
XLA Ops:
  0.0 84.8 %up_proj.1 = bf16[192,512]{1,0:T(8,128)(2,1)} custom-call(bf16[192,112]{1,0:T(8,128)(2,1)} %t_ref.1, bf16[448,512]{1,0:T(8,128)(2,1)} %w_ref.1, bf16[512]{0:T(512)(128)(2,1)} %b_ref.1), custom_call_target="tpu_custom_call" | custom-call | tf_op jit(solution)/shard_map/up_proj/pallas_call | solution.py:318
  84.8 1.6 %copy.5 = bf16[192,512]{1,0:T(8,128)(2,1)} copy(bf16[192,512]{1,0:T(8,128)(2,1)} %up_proj.1) | data formatting | bytes 393216

commit v5 on v3

--- a/solution.py
+++ b/solution.py
@@ -346,7 +346,7 @@
         ],
         name="up_proj",
         compiler_params=pltpu.CompilerParams(
-            collective_id=0, has_side_effects=True, vmem_limit_bytes=40 * 2**20
+            collective_id=0, has_side_effects=True, vmem_limit_bytes=60 * 2**20
         ),
     )(tokens, up_weight, up_bias)
 

time: 83.6 us -> 83.9 us (level)
  Pallas kernels: 80.2 us -> 82.1 us
  local copies, waits for them, and re-layouts: 3.17 us -> 1.62 us
    pallas_call x1, Pallas kernels: 80.2 us -> 82.1 us  [body(): pl.pallas_call(kernel, out_shape=jax.ShapeDtypeStruct((ROWS, 512), BF16),...]
    unnamed x7 -> x1, local copies, waits for them, and re-layouts: 3.17 us -> 1.62 us
where the time goes in v5:
time: 83.9 us; the launch traced here: 83.7 us
  Pallas kernels  82.1 us (98%)
  local copies, waits for them, and re-layouts  1.62 us (2%)
    pallas_call x1, Pallas kernels, body(): pl.pallas_call(kernel, out_shape=jax.ShapeDtypeStruct((ROWS, 512), BF16),...  82.1 us

profile of v5, /device:TPU:8, one launch (start us, length us, event | category | flops | bytes accessed | tf_op | source)
XLA Modules:
  0.0 83.7 jit_solution(11920287016737695928)
XLA Ops:
  0.0 82.1 %up_proj.1 = bf16[192,512]{1,0:T(8,128)(2,1)} custom-call(bf16[192,112]{1,0:T(8,128)(2,1)} %t_ref.1, bf16[448,512]{1,0:T(8,128)(2,1)} %w_ref.1, bf16[512]{0:T(512)(128)(2,1)} %b_ref.1), custom_call_target="tpu_custom_call" | custom-call | tf_op jit(solution)/shard_map/up_proj/pallas_call | solution.py:318
  82.1 1.6 %copy.5 = bf16[192,512]{1,0:T(8,128)(2,1)} copy(bf16[192,512]{1,0:T(8,128)(2,1)} %up_proj.1) | data formatting | bytes 393216

commit v6 on v5

--- a/solution.py
+++ b/solution.py
@@ -15,7 +15,7 @@
 FEAT = 112
 PART = 96
 STEPS = (
-    0, 1, 2, 5, 4, 3, 16, 96, 6, 17, 9, 18, 8, 7, 10, 19, 97, 34, 20, 35,
+    0, 1, 98, 2, 5, 4, 3, 16, 96, 6, 17, 9, 18, 8, 7, 10, 19, 97, 34, 20, 35,
     21, 11, 33, 32, 12, 37, 36, 23, 51, 22, 49, 38, 53, 50, 48, 13, 52, 39, 54, 24,
     55, 40, 25, 26, 42, 56, 41, 67, 27, 43, 66, 71, 15, 14, 70, 57, 58, 64, 65, 28,
     59, 44, 29, 30, 45, 46, 60, 68, 61, 62, 86, 75, 72, 87, 31, 47, 74, 73, 63, 76,
@@ -87,8 +87,8 @@
                 device_id=device(x, h, y, c, zl), device_id_type=MESH)
         return pltpu.make_async_copy(src, dst, local_sem.at[q])
 
-    def swap_all(run_remote, run_local):
-        for q in range(2):
+    def swap_all(run_remote, run_local, halves=(0, 1)):
+        for q in halves:
             for h in range(2):
                 here = (c == zh) & (c == h)
                 if run_local is not None:
@@ -128,7 +128,17 @@
         def _():
             t_local().start()
 
-    swap_all(lambda d: d.start(), lambda d: d.start())
+    swap_all(lambda d: d.start(), lambda d: d.start(), (0,))
+
+    @pl.when(c == zh)
+    def _():
+        swap_all(lambda d: d.start(), lambda d: d.start(), (1,))
+
+    def swap_second_half():
+        @pl.when(c != zh)
+        def _():
+            swap_all(lambda d: d.wait_send(), None, (0,))
+            swap_all(lambda d: d.start(), None, (1,))
 
     def w_copy(hops, way, part, half):
         rows = pl.ds(part * HALF, HALF)
@@ -285,6 +295,8 @@
             tree_step(i, kind - 2)
         elif i == 0:
             send_tokens()
+        elif i == 2:
+            swap_second_half()
         else:
             take_tokens()
 
@@ -295,7 +307,11 @@
     def _():
         t_copy(0).wait_send()
 
-    swap_all(lambda d: d.wait_send(), None)
+    swap_all(lambda d: d.wait_send(), None, (1,))
+
+    @pl.when(c == zh)
+    def _():
+        swap_all(lambda d: d.wait_send(), None, (0,))
 
     for i in range(PIECES):
         hops, way, half = piece_of(i)

time: 83.9 us -> 84.7 us (level)
  no operation moved by 1% of the time
where the time goes in v6:
time: 84.7 us; the launch traced here: 84.5 us
  Pallas kernels  82.9 us (98%)
  local copies, waits for them, and re-layouts  1.62 us (2%)
    pallas_call x1, Pallas kernels, body(): pl.pallas_call(kernel, out_shape=jax.ShapeDtypeStruct((ROWS, 512), BF16),...  82.9 us

profile of v6, /device:TPU:8, one launch (start us, length us, event | category | flops | bytes accessed | tf_op | source)
XLA Modules:
  0.0 84.5 jit_solution(7395987434106882962)
XLA Ops:
  0.0 82.9 %up_proj.1 = bf16[192,512]{1,0:T(8,128)(2,1)} custom-call(bf16[192,112]{1,0:T(8,128)(2,1)} %t_ref.1, bf16[448,512]{1,0:T(8,128)(2,1)} %w_ref.1, bf16[512]{0:T(512)(128)(2,1)} %b_ref.1), custom_call_target="tpu_custom_call" | custom-call | tf_op jit(solution)/shard_map/up_proj/pallas_call | solution.py:334
  82.9 1.6 %copy.5 = bf16[192,512]{1,0:T(8,128)(2,1)} copy(bf16[192,512]{1,0:T(8,128)(2,1)} %up_proj.1) | data formatting | bytes 393216

commit v7 on v5

--- a/solution.py
+++ b/solution.py
@@ -17,9 +17,9 @@
 STEPS = (
     0, 1, 2, 5, 4, 3, 16, 96, 6, 17, 9, 18, 8, 7, 10, 19, 97, 34, 20, 35,
     21, 11, 33, 32, 12, 37, 36, 23, 51, 22, 49, 38, 53, 50, 48, 13, 52, 39, 54, 24,
-    55, 40, 25, 26, 42, 56, 41, 67, 27, 43, 66, 71, 15, 14, 70, 57, 58, 64, 65, 28,
-    59, 44, 29, 30, 45, 46, 60, 68, 61, 62, 86, 75, 72, 87, 31, 47, 74, 73, 63, 76,
-    84, 69, 77, 78, 88, 83, 80, 89, 85, 79, 82, 81,
+    55, 40, 25, 26, 42, 56, 41, 27, 43, 15, 14, 67, 57, 58, 66, 71, 28, 59, 44, 70,
+    29, 30, 45, 64, 46, 65, 60, 61, 62, 31, 68, 47, 63, 75, 72, 86, 74, 73, 87, 76,
+    69, 77, 78, 84, 79, 88, 83, 80, 89, 85, 82, 81,
 )
 DEEP = {
     4: (1, -1, 0, 0), 2: (1, -1, 0, 0), 5: (1, 1, 0, 0),

time: 83.9 us -> 84.1 us (level)
  no operation moved by 1% of the time
where the time goes in v7:
time: 84.1 us; the launch traced here: 83.9 us
  Pallas kernels  82.3 us (98%)
  local copies, waits for them, and re-layouts  1.62 us (2%)
    pallas_call x1, Pallas kernels, body(): pl.pallas_call(kernel, out_shape=jax.ShapeDtypeStruct((ROWS, 512), BF16),...  82.3 us

profile of v7, /device:TPU:8, one launch (start us, length us, event | category | flops | bytes accessed | tf_op | source)
XLA Modules:
  0.0 83.9 jit_solution(16654454808802088739)
XLA Ops:
  0.0 82.3 %up_proj.1 = bf16[192,512]{1,0:T(8,128)(2,1)} custom-call(bf16[192,112]{1,0:T(8,128)(2,1)} %t_ref.1, bf16[448,512]{1,0:T(8,128)(2,1)} %w_ref.1, bf16[512]{0:T(512)(128)(2,1)} %b_ref.1), custom_call_target="tpu_custom_call" | custom-call | tf_op jit(solution)/shard_map/up_proj/pallas_call | solution.py:318
  82.3 1.6 %copy.5 = bf16[192,512]{1,0:T(8,128)(2,1)} copy(bf16[192,512]{1,0:T(8,128)(2,1)} %up_proj.1) | data formatting | bytes 393216
